TPU v7x, 32 devices: a whole 2x2x4 slice. The times are simulated.
32 devices in a mesh: region: 4 (over y, core), group: 8 (over z, x).
Axes of the slice: x: 2, y: 2, z: 4, core: 2. Of those that a mesh axis runs over, the one named last changes fastest.
Arguments:
- phi: bfloat16 [1024, 12288], P('group', 'region'), may hold values from -6 to 6
- hphi: bfloat16 [1024, 12288], P('group', 'region'), may hold values from -6 to 6
- extents: int32 [1024, 2], P('group'), may hold values from 0 to 12288, as said below
- columns: int32 [8, 3], replicated, may hold values from 0 to 7, as said below
- kernel: bfloat16 [8, 3, 128, 128], replicated, may hold values from -0.3125 to 0.3125
Outputs:
- gradient: bfloat16 [1024, 12288], P('group', 'region')
- lagrange: float32 [8, 3, 128, 128], P('group')
Inputs may be any that keep to these rules, and one draw needn't show every extreme that they name: extents[f, 0] < extents[f, 1]; each region starts at or before point 12288 - 3 * 3072 and spans 9216 to 18432 points before it is cut at the grid's end. Each block row lists 3 distinct block columns, the first being the row itself.
All inputs are finite; a program needn't handle non-finite values.
Results may differ from a plain program's by a relative error of at most 0.005.
Values may be sent and summed in bfloat16 or wider, within the bound.
A program may use at most 128 MiB of HBM per device.

v0:
```python
import jax
import jax.numpy as jnp
from jax import lax
from jax.sharding import PartitionSpec as P


def shards(phi, hphi, extents, columns, kernel):
    own_rows, width = phi.shape
    point = lax.axis_index("region") * width + lax.broadcasted_iota(jnp.int32, (own_rows, width), 1)
    inside = (point >= extents[:, 0:1]) & (point < extents[:, 1:2])
    zero = jnp.zeros((), jnp.bfloat16)
    phi_loc = jnp.where(inside, phi, zero)
    hphi_loc = jnp.where(inside, hphi, zero)
    phi_grid, hphi_grid = (
        lax.all_to_all(phi_loc, "group", split_axis=1, concat_axis=0, tiled=True),
        lax.all_to_all(hphi_loc, "group", split_axis=1, concat_axis=0, tiled=True),
    )
    nfun, npts = phi_grid.shape
    block = kernel.shape[2]
    nblocks = nfun // block
    owned_blocks = nblocks // lax.axis_size("group")
    shifted = (hphi_grid.astype(jnp.float32) + 0.5 * phi_grid.astype(jnp.float32)).astype(
        jnp.bfloat16
    )
    phi_rows = phi_grid.reshape(nblocks, block, npts)
    hphi_rows = hphi_grid.reshape(nblocks, block, npts)
    shift_rows = shifted.reshape(nblocks, block, npts)
    identity = jnp.eye(block, dtype=jnp.float32)
    volume = 1.0 / width
    total = lax.psum(
        jnp.einsum(
            "aip,ajkp->ajik", phi_rows, shift_rows[columns], preferred_element_type=jnp.float32
        ),
        ("region", "group"),
    )
    full = (total * volume).at[:, 0].add(-0.5 * identity)
    lagrange_low = full.astype(jnp.bfloat16)
    owned = lax.dynamic_slice_in_dim(full, lax.axis_index("group") * owned_blocks, owned_blocks, 0)
    images = hphi_rows[columns]
    values = phi_rows[columns]
    raw = jnp.einsum("ajik,ajkp->aip", kernel, images, preferred_element_type=jnp.float32)
    raw = raw - jnp.einsum(
        "ajik,ajkp->aip", lagrange_low, values, preferred_element_type=jnp.float32
    )
    raw = raw.reshape(nfun, npts).astype(jnp.bfloat16)
    returned = lax.all_to_all(raw, "group", split_axis=0, concat_axis=1, tiled=True)
    gradient = jnp.where(inside, returned, zero)
    return (gradient, owned)


def solution(mesh):
    return jax.shard_map(
        shards,
        mesh=mesh,
        in_specs=(P("group", "region"), P("group", "region"), P("group", None), P(), P()),
        out_specs=(P("group", "region"), P("group", None, None, None)),
        check_vma=False,
    )
```

profile of v0, /device:TPU:0, one launch (start us, length us, event | category | flops | bytes accessed | tf_op | source)
XLA Modules:
  0.0 240.0 jit_solution(5557465177857803256)
XLA Ops:
  7.2 0.0 copy-start
  7.2 0.0 copy-start.3
  7.2 0.8 slice_bitcast_fusion.1
  8.0 1.5 copy.13
  9.5 0.0 copy-done.3
  9.5 0.4 copy.17
  9.9 2.1 fusion.2
  12.1 2.3 copy.18
  14.4 7.3 %all-to-all-start.1 = ((bf16[128,8,384]{2,0,1:T(8,128)(2,1)}), bf16[128,8,384]{2,0,1:T(8,128)(2,1)S(1)}, u32[]{:S(2)}, u32[]{:S(2)}) async-start(bf16[128,8,384]{2,0,1:T(8,128)(2,1)} %copy.18), calls=%async_computation.1 | async-start | bytes 1572864 | tf_op jit(solution)/shard_map/all_to_all | solution.py:15
  21.6 0.0 copy-start.4
  21.6 1.2 copy.14
  22.8 19.0 %all-to-all-done.1 = bf16[128,8,384]{2,0,1:T(8,128)(2,1)S(1)} async-done(((bf16[128,8,384]{2,0,1:T(8,128)(2,1)}), bf16[128,8,384]{2,0,1:T(8,128)(2,1)S(1)}, u32[]{:S(2)}, u32[]{:S(2)}) %all-to-all-start.1) | async-done | bytes 786464 | tf_op jit(solution)/shard_map/all_to_all | solution.py:15
  41.8 3.6 %all-to-all-start = ((bf16[128,8,384]{2,0,1:T(8,128)(2,1)}), bf16[128,8,384]{2,0,1:T(8,128)(2,1)S(1)}, u32[]{:S(2)}, u32[]{:S(2)}) async-start(bf16[128,8,384]{2,0,1:T(8,128)(2,1)} %copy.14), calls=%async_computation | async-start | bytes 1572864 | tf_op jit(solution)/shard_map/all_to_all | solution.py:16
  45.4 0.0 all-reduce.2.cloned.1.call-start
  45.4 0.0 copy-done.4
  45.4 0.1 copy.15
  45.5 0.1 reshape.54
  45.6 20.1 %all-to-all-done = bf16[128,8,384]{2,0,1:T(8,128)(2,1)S(1)} async-done(((bf16[128,8,384]{2,0,1:T(8,128)(2,1)}), bf16[128,8,384]{2,0,1:T(8,128)(2,1)S(1)}, u32[]{:S(2)}, u32[]{:S(2)}) %all-to-all-start) | async-done | bytes 786464 | tf_op jit(solution)/shard_map/all_to_all | solution.py:16
  65.7 0.2 add_convert_fusion
  66.0 2.4 %gather_fusion.1 = bf16[24,128,384]{2,1,0:T(8,128)(2,1)} fusion(bf16[8,128,384]{2,1,0:T(8,128)(2,1)S(1)} %add_convert_fusion, s32[1024]{0:T(1024)S(1)} %pad_clamp_fusion), kind=kCustom, calls=%fused_computation.1 | custom fusion | bytes 4718688 | tf_op jit(solution)/shard_map/gather | solution.py:32
  68.4 3.6 %convolution_bitcast_fusion = f32[8,3,128,128]{2,3,1,0:T(8,128)} fusion(bf16[8,3,128,384]{3,2,1,0:T(8,128)(2,1)} %bitcast.42, bf16[128,8,384]{2,0,1:T(8,128)(2,1)S(1)} %all-to-all-done.1), kind=kOutput, calls=%fused_computation.7 | convolution fusion | flops 301989888 | bytes 4718592 | tf_op jit(solution)/shard_map/aip,ajkp->ajik/dot_general | solution.py:31
  72.0 0.0 all-reduce.2.cloned.1.call-update
  72.1 2.4 %gather_fusion.2 = bf16[24,128,384]{2,1,0:T(8,128)(2,1)} fusion(bf16[8,128,384]{2,1,0:T(8,128)(2,1)S(1)} %bitcast.38, s32[1024]{0:T(1024)S(1)} %pad_clamp_fusion), kind=kCustom, calls=%fused_computation.2 | custom fusion | bytes 4718688 | tf_op jit(solution)/shard_map/gather | solution.py:40
  74.5 2.4 %gather_fusion = bf16[24,128,384]{2,1,0:T(8,128)(2,1)} fusion(bf16[8,128,384]{2,1,0:T(8,128)(2,1)S(1)} %bitcast.39, s32[1024]{0:T(1024)S(1)} %pad_clamp_fusion), kind=kCustom, calls=%fused_computation | custom fusion | bytes 4718688 | tf_op jit(solution)/shard_map/gather | solution.py:39
  76.9 0.0 copy-done
  76.9 3.8 %fusion.8 = f32[8,384,128,1]{2,1,3,0:T(8,128)} fusion(bf16[8,3,128,384]{3,2,1,0:T(8,128)(2,1)} %bitcast.41, bf16[8,3,128,128]{3,2,1,0:T(8,128)(2,1)S(1)} %copy-done), kind=kOutput, calls=%fused_computation.24 | convolution fusion | flops 301989888 | bytes 4718592 | tf_op jit(solution)/shard_map/ajik,ajkp->aip/dot_general | solution.py:41
  80.7 122.4 %all-reduce.2.cloned.1.call-done = f32[8,3,128,128]{2,3,1,0:T(8,128)} async-done(((f32[8,3,128,128]{2,3,1,0:T(8,128)}), f32[8,3,128,128]{2,3,1,0:T(8,128)}) %all-reduce.2.cloned.1.call-update) | async-done | bytes 1572880 | tf_op jit(solution)/shard_map/psum | solution.py:30
  203.1 0.0 copy-start.1
  203.2 0.0 copy-start.2
  203.2 1.7 broadcast_multiply_fusion
  204.9 0.1 fusion.6
  205.0 0.3 copy-done.1
  205.3 0.5 copy-done.2
  205.7 1.8 fusion
  207.6 4.4 %all-to-all-start.2 = ((bf16[8,128,384]{1,2,0:T(8,128)(2,1)}), bf16[8,128,384]{1,2,0:T(8,128)(2,1)S(1)}, u32[]{:S(2)}, u32[]{:S(2)}) async-start(bf16[8,128,384]{1,2,0:T(8,128)(2,1)} %fusion), calls=%async_computation.2 | async-start | bytes 1572864 | tf_op jit(solution)/shard_map/all_to_all | solution.py:46
  212.0 0.8 copy.22
  212.8 17.9 %all-to-all-done.2 = bf16[8,128,384]{1,2,0:T(8,128)(2,1)S(1)} async-done(((bf16[8,128,384]{1,2,0:T(8,128)(2,1)}), bf16[8,128,384]{1,2,0:T(8,128)(2,1)S(1)}, u32[]{:S(2)}, u32[]{:S(2)}) %all-to-all-start.2) | async-done | bytes 786464 | tf_op jit(solution)/shard_map/all_to_all | solution.py:46
  230.6 1.4 fusion.1
  232.0 1.2 copy.21
  (5 shorter events, 0.0 us)
Async XLA Ops:
  7.2 69.8 %copy-start = (bf16[8,3,128,128]{3,2,1,0:T(8,128)(2,1)S(1)}, bf16[8,3,128,128]{3,2,1,0:T(8,128)(2,1)}, u32[]{:S(2)}) copy-start(bf16[8,3,128,128]{3,2,1,0:T(8,128)(2,1)} %param.11) | copy-start | bytes 2359300
  7.2 2.4 copy-start.3
  14.4 27.4 %all-to-all-start.1 = ((bf16[128,8,384]{2,0,1:T(8,128)(2,1)}), bf16[128,8,384]{2,0,1:T(8,128)(2,1)S(1)}, u32[]{:S(2)}, u32[]{:S(2)}) async-start(bf16[128,8,384]{2,0,1:T(8,128)(2,1)} %copy.18), calls=%async_computation.1 | async-start | bytes 1572864 | tf_op jit(solution)/shard_map/all_to_all | solution.py:15
  21.6 23.8 %copy-start.4 = (s32[8,3]{0,1:T(4,128)S(1)}, s32[8,3]{0,1:T(4,128)}, u32[]{:S(2)}) copy-start(s32[8,3]{0,1:T(4,128)} %param.10) | copy-start | bytes 292
  41.8 23.9 %all-to-all-start = ((bf16[128,8,384]{2,0,1:T(8,128)(2,1)}), bf16[128,8,384]{2,0,1:T(8,128)(2,1)S(1)}, u32[]{:S(2)}, u32[]{:S(2)}) async-start(bf16[128,8,384]{2,0,1:T(8,128)(2,1)} %copy.14), calls=%async_computation | async-start | bytes 1572864 | tf_op jit(solution)/shard_map/all_to_all | solution.py:16
  45.4 157.8 %all-reduce.2.cloned.1.call-start = ((), (), s32[]{:S(2)}) async-start(), calls=%async_computation.3 | async-start | bytes 3145728 | tf_op jit(solution)/shard_map/psum | solution.py:30
  203.1 2.1 copy-start.1
  203.2 2.6 %copy-start.2 = (f32[8,384,128,1]{2,1,3,0:T(8,128)S(1)}, f32[8,384,128,1]{2,1,3,0:T(8,128)}, u32[]{:S(2)}) copy-start(f32[8,384,128,1]{2,1,3,0:T(8,128)} %fusion.8) | copy-start | bytes 4718596
  207.6 23.1 %all-to-all-start.2 = ((bf16[8,128,384]{1,2,0:T(8,128)(2,1)}), bf16[8,128,384]{1,2,0:T(8,128)(2,1)S(1)}, u32[]{:S(2)}, u32[]{:S(2)}) async-start(bf16[8,128,384]{1,2,0:T(8,128)(2,1)} %fusion), calls=%async_computation.2 | async-start | bytes 1572864 | tf_op jit(solution)/shard_map/all_to_all | solution.py:46
Sparse Core Ops, SparseCore 0:
  72.2 130.9 all-reduce.1
where the time goes:
time: 240 us
  waiting for transfers between devices  179 us (75%)
  local copies, waits for them, and re-layouts  16.3 us (7%)
  starting transfers between devices  15.2 us (6%)
  between operations  14.1 us (6%)
  matrix products  9.25 us (4%)
  other arithmetic  5.58 us (2%)
    psum x1, waiting for transfers between devices, shards(): lax.psum(jnp.einsum('aip,ajkp->ajik', phi_rows, shift_rows[columns], pref...  122 us
    all_to_all x1, waiting for transfers between devices, shards(): lax.all_to_all(hphi_loc, 'group', split_axis=1, concat_axis=0, tiled=True)  20.1 us
    all_to_all x1, waiting for transfers between devices, shards(): lax.all_to_all(phi_loc, 'group', split_axis=1, concat_axis=0, tiled=True)  19 us
    all_to_all x1, waiting for transfers between devices, shards(): lax.all_to_all(raw, 'group', split_axis=0, concat_axis=1, tiled=True)  17.9 us
    all_to_all x1, starting transfers between devices, shards(): lax.all_to_all(phi_loc, 'group', split_axis=1, concat_axis=0, tiled=True)  7.25 us
  transfers between devices with their start and end apart: 4, of which 4 were waited for; matrix products, arithmetic and copies ran while one was open for 5% of the time, Pallas kernels for 0%

commit v1 on v0

v1 whole, which is shorter than its diff:
```python
import functools

import jax
import jax.numpy as jnp
from jax import lax
from jax.experimental import pallas as pl
from jax.experimental.pallas import tpu as pltpu
from jax.sharding import PartitionSpec as P

F32 = jnp.float32
BF16 = jnp.bfloat16


def body(n, nreg, phi, hphi, ext, col, ker, grad, lag,
         src, grid, shift, part, cbuf, ybuf, red, gbuf, low, fbuf, kh, ret,
         as_, ar, cs, cr, ys, yr, gs, gr, ls, lr, fs, fr, lys, lyr, lcs, lcr, bs, br):
    rows, width = phi.shape
    depth = width // n
    nbr = col.shape[1]
    pairs = nreg // 2
    slab = rows // nreg
    me = lax.axis_index("group")
    r = lax.axis_index("region")
    q = r // 2
    c = r % 2
    partner = 2 * q + 1 - c

    def to_group(a, b, s1, s2, k):
        return pltpu.make_async_remote_copy(
            src_ref=a, dst_ref=b, send_sem=s1, recv_sem=s2,
            device_id={"group": k}, device_id_type=pl.DeviceIdType.MESH)

    def to_region(a, b, s1, s2, k):
        return pltpu.make_async_remote_copy(
            src_ref=a, dst_ref=b, send_sem=s1, recv_sem=s2,
            device_id={"region": k}, device_id_type=pl.DeviceIdType.MESH)

    def each(lo, hi, f):
        def step(s, carry):
            f(s)
            return carry
        lax.fori_loop(lo, hi, step, 0)

    up = lambda s: lax.rem(me + s, n)
    down = lambda s: lax.rem(me + n - s, n)
    rup = lambda t: lax.rem(r + t, nreg)
    qup = lambda t: lax.rem(q + t, pairs)

    barrier = pltpu.get_barrier_semaphore()
    each(1, n, lambda s: pl.semaphore_signal(
        barrier, inc=1, device_id={"group": up(s)}, device_id_type=pl.DeviceIdType.MESH))
    each(1, nreg, lambda t: pl.semaphore_signal(
        barrier, inc=1, device_id={"region": rup(t)}, device_id_type=pl.DeviceIdType.MESH))

    first = ext[:, 0:1]
    last = ext[:, 1:2]

    def inside(k):
        point = r * width + k * depth + lax.broadcasted_iota(jnp.int32, (rows, depth), 1)
        return (point >= first) & (point < last)

    def cut(k):
        return pl.ds(pl.multiple_of(k * depth, 128), depth)

    def masked(ref, k):
        return jnp.where(inside(k), ref[:, cut(k)].astype(F32), 0.0).astype(BF16)

    def shifted(k):
        shift[k] = (grid[k, 1].astype(F32) + 0.5 * grid[k, 0].astype(F32)).astype(BF16)

    grid[me, 0] = masked(phi, me)
    grid[me, 1] = masked(hphi, me)
    shifted(me)
    pl.semaphore_wait(barrier, n - 1 + nreg - 1)

    def out_copy(k):
        return to_group(src.at[k], grid.at[me], as_.at[k], ar.at[me], k)

    def send_out(s):
        k = up(s)
        src[k, 0] = masked(phi, k)
        src[k, 1] = masked(hphi, k)
        out_copy(k).start()
    each(1, n, send_out)

    def take_in(s):
        k = down(s)
        to_group(src.at[k], grid.at[k], as_.at[k], ar.at[k], k).wait_recv()
        shifted(k)
    each(1, n, take_in)

    def core_copy(p, a):
        return to_region(part.at[1 - c, p, a], cbuf.at[p, a], cs.at[p, a], cr.at[p, a], partner)

    def partial(s):
        a = up(s)
        left = grid[a, 0]
        for j in range(nbr):
            res = lax.dot_general(left, shift[col[a, j]], (((1,), (1,)), ((), ())),
                                  preferred_element_type=F32)
            for i in range(nreg):
                part[i % 2, i // 2, a, j] = res[i * slab:(i + 1) * slab]
        each(1, pairs + 1, lambda t: core_copy(qup(t), a).start())
    each(1, n + 1, partial)

    def y_copy(p, a):
        return to_region(part.at[c, p, a], ybuf.at[q, a], ys.at[p, a], yr.at[q, a], 2 * p + c)

    def y_wait(p, a):
        to_region(part.at[c, p, a], ybuf.at[p, a], ys.at[p, a], yr.at[p, a], 2 * p + c).wait_recv()

    def forward(s):
        a = up(s)

        def one(t):
            p = qup(t)
            core_copy(p, a).wait_recv()
            part[c, p, a] = part[c, p, a] + cbuf[p, a]
            y_copy(p, a).start()
        each(1, pairs, one)
    each(1, n + 1, forward)

    def red_copy(k):
        return to_group(red.at[k], gbuf.at[me], gs.at[k], gr.at[me], k)

    def reduce_one(a):
        total = jnp.zeros((rows, depth), F32)
        for j in range(nbr):
            total = total + jnp.dot(ker[a, j], grid[col[a, j], 1], preferred_element_type=F32)
        kh[a] = total
        core_copy(q, a).wait_recv()
        red[a] = part[c, q, a] + cbuf[q, a]

        def one(t):
            p = qup(t)
            y_wait(p, a)
            red[a] = red[a] + ybuf[p, a]
        each(1, pairs, one)

    def reduce_send(s):
        a = up(s)
        reduce_one(a)
        red_copy(a).start()
    each(1, n, reduce_send)
    reduce_one(me)

    def gather_sum(s):
        k = down(s)
        to_group(red.at[k], gbuf.at[k], gs.at[k], gr.at[k], k).wait_recv()
        red[me] = red[me] + gbuf[k]
    each(1, n, gather_sum)

    slot = lax.broadcasted_iota(jnp.int32, (nbr, slab, rows), 0)
    row = r * slab + lax.broadcasted_iota(jnp.int32, (nbr, slab, rows), 1)
    column = lax.broadcasted_iota(jnp.int32, (nbr, slab, rows), 2)
    eye = jnp.where((slot == 0) & (row == column), 0.5, 0.0)
    full = red[me] * (1.0 / width) - eye
    fbuf[r] = full
    low[c, q, me] = full.astype(BF16)

    def low_copy(k):
        return to_group(low.at[c, q, me], low.at[c, q, me], ls.at[k], lr.at[me], k)

    def low_wait(k):
        to_group(low.at[c, q, k], low.at[c, q, k], ls.at[k], lr.at[k], k).wait_recv()

    def ly_copy(p, k):
        return to_region(low.at[c, q, k], low.at[c, q, k], lys.at[p, k], lyr.at[q, k], 2 * p + c)

    def ly_wait(p, k):
        to_region(low.at[c, p, k], low.at[c, p, k], lys.at[p, k], lyr.at[p, k],
                  2 * p + c).wait_recv()

    def lc_copy(p, k):
        return to_region(low.at[c, p, k], low.at[c, p, k], lcs.at[p, k], lcr.at[p, k], partner)

    def lc_wait(p, k):
        to_region(low.at[1 - c, p, k], low.at[1 - c, p, k], lcs.at[p, k], lcr.at[p, k],
                  partner).wait_recv()

    def full_copy(i):
        return to_region(fbuf.at[r], fbuf.at[r], fs.at[i], fr.at[r], i)

    each(1, n, lambda s: low_copy(up(s)).start())

    def spread(s):
        k = down(s)
        low_wait(k)
        each(1, pairs, lambda t: ly_copy(qup(t), k).start())
        lc_copy(q, k).start()
    each(1, n, spread)
    each(1, pairs, lambda t: ly_copy(qup(t), me).start())
    lc_copy(q, me).start()
    each(1, nreg, lambda t: full_copy(rup(t)).start())

    def relay(s):
        k = down(s)

        def one(t):
            p = qup(t)
            ly_wait(p, k)
            lc_copy(p, k).start()
        each(1, pairs, one)
    each(1, n + 1, relay)

    def back_copy(a):
        return to_group(shift.at[a], ret.at[me], bs.at[a], br.at[me], a)

    def descend(a):
        each(0, pairs, lambda p: lc_wait(p, a))
        total = kh[a]
        for j in range(nbr):
            block = jnp.concatenate([low[i % 2, i // 2, a, j] for i in range(nreg)], axis=0)
            total = total - jnp.dot(block, grid[col[a, j], 0], preferred_element_type=F32)
        return total.astype(BF16)

    def send_back(s):
        a = down(s)
        shift[a] = descend(a)
        back_copy(a).start()
    each(1, n, send_back)

    def store(k, value):
        grad[:, cut(k)] = jnp.where(inside(k), value.astype(F32), 0.0).astype(BF16)

    store(me, descend(me))

    def finish(s):
        k = up(s)
        to_group(shift.at[k], ret.at[k], bs.at[k], br.at[k], k).wait_recv()
        store(k, ret[k])
    each(1, n, finish)

    def full_wait(t):
        i = rup(t)
        to_region(fbuf.at[i], fbuf.at[i], fs.at[i], fr.at[i], i).wait_recv()
    each(1, nreg, full_wait)
    for i in range(nreg):
        for j in range(nbr):
            lag[0, j, i * slab:(i + 1) * slab, :] = fbuf[i, j]

    def drain(s):
        k = up(s)
        out_copy(k).wait_send()
        red_copy(k).wait_send()
        low_copy(k).wait_send()
        back_copy(k).wait_send()
    each(1, n, drain)
    each(1, nreg, lambda t: full_copy(rup(t)).wait_send())

    def drain_region(a):
        def own(p):
            core_copy(p, a).wait_send()
            lc_copy(p, a).wait_send()

        def other(t):
            y_copy(qup(t), a).wait_send()
            ly_copy(qup(t), a).wait_send()
        each(0, pairs, own)
        each(1, pairs, other)
    each(0, n, drain_region)


def shards(phi, hphi, extents, columns, kernel):
    rows, width = phi.shape
    n = lax.axis_size("group")
    nreg = lax.axis_size("region")
    nbr = columns.shape[1]
    depth = width // n
    pairs = nreg // 2
    slab = rows // nreg
    dma = pltpu.SemaphoreType.DMA
    vmem = pl.BlockSpec(memory_space=pltpu.VMEM)
    smem = pl.BlockSpec(memory_space=pltpu.SMEM)
    return pl.pallas_call(
        functools.partial(body, n, nreg),
        out_shape=(jax.ShapeDtypeStruct((rows, width), BF16),
                   jax.ShapeDtypeStruct((1, nbr, rows, rows), F32)),
        in_specs=[vmem, vmem, vmem, smem, vmem],
        out_specs=(vmem, vmem),
        scratch_shapes=[
            pltpu.VMEM((n, 2, rows, depth), BF16),
            pltpu.VMEM((n, 2, rows, depth), BF16),
            pltpu.VMEM((n, rows, depth), BF16),
            pltpu.VMEM((2, pairs, n, nbr, slab, rows), F32),
            pltpu.VMEM((pairs, n, nbr, slab, rows), F32),
            pltpu.VMEM((pairs, n, nbr, slab, rows), F32),
            pltpu.VMEM((n, nbr, slab, rows), F32),
            pltpu.VMEM((n, nbr, slab, rows), F32),
            pltpu.VMEM((2, pairs, n, nbr, slab, rows), BF16),
            pltpu.VMEM((nreg, nbr, slab, rows), F32),
            pltpu.VMEM((n, rows, depth), F32),
            pltpu.VMEM((n, rows, depth), BF16),
            dma((n,)), dma((n,)),
            dma((pairs, n)), dma((pairs, n)),
            dma((pairs, n)), dma((pairs, n)),
            dma((n,)), dma((n,)),
            dma((n,)), dma((n,)),
            dma((nreg,)), dma((nreg,)),
            dma((pairs, n)), dma((pairs, n)),
            dma((pairs, n)), dma((pairs, n)),
            dma((n,)), dma((n,)),
        ],
        compiler_params=pltpu.CompilerParams(
            collective_id=0, has_side_effects=True, vmem_limit_bytes=60 * 1024 * 1024),
        cost_estimate=pl.CostEstimate(
            flops=6 * n * nbr * rows * rows * depth, bytes_accessed=8 * rows * width,
            transcendentals=0),
    )(phi, hphi, extents, columns, kernel)


def solution(mesh):
    return jax.shard_map(
        shards,
        mesh=mesh,
        in_specs=(P("group", "region"), P("group", "region"), P("group", None), P(), P()),
        out_specs=(P("group", "region"), P("group", None, None, None)),
        check_vma=False,
    )
```

time: 240 us -> 98.7 us (0.41)
  waiting for transfers between devices: 179 us -> 0 us
  Pallas kernels: 0 us -> 92.9 us
  starting transfers between devices: 15.2 us -> 0 us
  between operations: 14.1 us -> 0.66 us
  local copies, waits for them, and re-layouts: 16.3 us -> 4.88 us
  matrix products: 9.25 us -> 0 us
  other arithmetic: 5.58 us -> 0 us
    psum x1 -> x0, waiting for transfers between devices: 122 us -> none  [shards(): lax.psum(jnp.einsum('aip,ajkp->ajik', phi_rows, shift_rows[columns], pref...]
    pallas_call x0 -> x1, Pallas kernels: none -> 92.9 us  [shards(): pl.pallas_call(functools.partial(body, n, nreg), out_shape=(jax.ShapeDtyp...]
    all_to_all x3 -> x0, waiting for transfers between devices: 57 us -> none  [the longest x1 20.1 us: shards(): lax.all_to_all(hphi_loc, 'group', split_axis=1, concat_axis=0, tiled=True)]
    all_to_all x3 -> x0, starting transfers between devices: 15.2 us -> none  [the longest x1 7.25 us: shards(): lax.all_to_all(phi_loc, 'group', split_axis=1, concat_axis=0, tiled=True)]
    dot_general x3 -> x0, matrix products: 9.25 us -> none  [the longest x1 3.79 us: shards(): jnp.einsum('ajik,ajkp->aip', kernel, images, preferred_element_type=jnp.f...]
    gather x3 -> x0, local copies, waits for them, and re-layouts: 7.26 us -> none  [the longest x1 2.42 us: shards(): shift_rows[columns]]
    select_n x3 -> x0, other arithmetic: 3.5 us -> none  [the longest x1 2.14 us: shards(): phi_loc = jnp.where(inside, phi, zero)]
    all_to_all x2 -> x0, local copies, waits for them, and re-layouts: 3.47 us -> none  [the longest x1 2.3 us: shards(): lax.all_to_all(phi_loc, 'group', split_axis=1, concat_axis=0, tiled=True)]
  transfers between devices with their start and end apart: 4 -> 0, of which waited for: 4 -> 0; matrix products, arithmetic and copies ran while one was open for 5% -> 0% of each run, Pallas kernels for 0% -> 0%
where the time goes in v1:
time: 98.7 us; the launch traced here: 98.5 us
  Pallas kernels  92.9 us (94%)
  local copies, waits for them, and re-layouts  4.88 us (5%)
    pallas_call x1, Pallas kernels, shards(): pl.pallas_call(functools.partial(body, n, nreg), out_shape=(jax.ShapeDtyp...  92.9 us
    unnamed x8, local copies, waits for them, and re-layouts  4.88 us

profile of v1, /device:TPU:0, one launch (start us, length us, event | category | flops | bytes accessed | tf_op | source)
XLA Modules:
  0.0 98.5 jit_solution(9235978344982140881)
XLA Ops:
  0.6 0.0 copy-start.1
  0.6 1.4 %copy.8.col = s32[8,3]{1,0:T(8,128)} copy(s32[8,3]{0,1:T(4,128)} %param.8) | data formatting | bytes 192 | tf_op args[3]
  2.0 0.0 copy-done.1
  2.0 0.7 copy.7.ext
  2.7 92.9 %shard_map.68 = (bf16[128,3072]{1,0:T(8,128)(2,1)}, f32[1,3,128,128]{3,2,1,0:T(8,128)}) custom-call(bf16[128,3072]{1,0:T(8,128)(2,1)} %phi.1, bf16[128,3072]{1,0:T(8,128)(2,1)} %hphi.1, s32[128,2]{1,0:T(8,128)} %copy.7.ext, s32[8,3]{1,0:T(8,128)} %copy.8.col, bf16[8,3,128,128]{3,2,1,0:T(8,128)(2,1)} %ker.1), custom_call_target="tpu_custom_call" | custom-call | flops 905969664 | bytes 3145728 | tf_op jit(solution)/shard_map/pallas_call | solution.py:275
  95.7 0.0 copy-start
  95.7 2.1 %copy.11 = bf16[128,3072]{1,0:T(8,128)(2,1)} copy(bf16[128,3072]{1,0:T(8,128)(2,1)} %get-tuple-element.4) | data formatting | bytes 1572864
  97.8 0.0 copy-done
  97.8 0.7 copy.12
Async XLA Ops:
  0.6 1.4 %copy-start.1 = (s32[128,2]{0,1:T(2,128)S(1)}, s32[128,2]{0,1:T(2,128)}, u32[]{:S(2)}) copy-start(s32[128,2]{0,1:T(2,128)} %param.7) | copy-start | bytes 3076
  95.7 2.1 %copy-start = (f32[1,3,128,128]{3,2,1,0:T(8,128)S(1)}, f32[1,3,128,128]{3,2,1,0:T(8,128)}, u32[]{:S(2)}) copy-start(f32[1,3,128,128]{3,2,1,0:T(8,128)} %get-tuple-element.5) | copy-start | bytes 589828

commit v2 on v1

--- a/solution.py
+++ b/solution.py
@@ -11,12 +11,12 @@
 BF16 = jnp.bfloat16
 
 
-def body(n, nreg, phi, hphi, ext, col, ker, grad, lag,
-         src, grid, shift, part, cbuf, ybuf, red, gbuf, low, fbuf, kh, ret,
+def body(n, nreg, phi, hphi, ext, colh, ker, grad, lag,
+         col, colsem, ysend, rsend, src, gridp, gridh, shift, part, cbuf, ybuf, red, gbuf, low, fbuf, kh, ret,
          as_, ar, cs, cr, ys, yr, gs, gr, ls, lr, fs, fr, lys, lyr, lcs, lcr, bs, br):
     rows, width = phi.shape
     depth = width // n
-    nbr = col.shape[1]
+    nbr = col.shape[0]
     pairs = nreg // 2
     slab = rows // nreg
     me = lax.axis_index("group")
@@ -41,8 +41,18 @@
             return carry
         lax.fori_loop(lo, hi, step, 0)
 
-    up = lambda s: lax.rem(me + s, n)
-    down = lambda s: lax.rem(me + n - s, n)
+    half = n // 2
+    base = me // half * half
+    place = me % half
+
+    def up(s):
+        start = jnp.where(s <= half, half - base, base)
+        return start + lax.rem(place + jnp.where(s <= half, s - 1, s - half), half)
+
+    def down(s):
+        start = jnp.where(s <= half, half - base, base)
+        return start + lax.rem(place + n - jnp.where(s <= half, s - 1, s - half), half)
+
     rup = lambda t: lax.rem(r + t, nreg)
     qup = lambda t: lax.rem(q + t, pairs)
 
@@ -52,8 +62,11 @@
     each(1, nreg, lambda t: pl.semaphore_signal(
         barrier, inc=1, device_id={"region": rup(t)}, device_id_type=pl.DeviceIdType.MESH))
 
-    first = ext[:, 0:1]
-    last = ext[:, 1:2]
+    fetch = pltpu.make_async_copy(colh, col, colsem)
+    fetch.start()
+    bounds = jnp.transpose(jnp.concatenate([ext[...]] * 4, axis=0))
+    first = bounds[:, 0:1]
+    last = bounds[:, 1:2]
 
     def inside(k):
         point = r * width + k * depth + lax.broadcasted_iota(jnp.int32, (rows, depth), 1)
@@ -66,26 +79,42 @@
         return jnp.where(inside(k), ref[:, cut(k)].astype(F32), 0.0).astype(BF16)
 
     def shifted(k):
-        shift[k] = (grid[k, 1].astype(F32) + 0.5 * grid[k, 0].astype(F32)).astype(BF16)
-
-    grid[me, 0] = masked(phi, me)
-    grid[me, 1] = masked(hphi, me)
+        shift[k] = (gridh[k].astype(F32) + 0.5 * gridp[k].astype(F32)).astype(BF16)
+
+    gridp[me] = masked(phi, me)
+    gridh[me] = masked(hphi, me)
     shifted(me)
     pl.semaphore_wait(barrier, n - 1 + nreg - 1)
 
-    def out_copy(k):
-        return to_group(src.at[k], grid.at[me], as_.at[k], ar.at[me], k)
-
-    def send_out(s):
-        k = up(s)
-        src[k, 0] = masked(phi, k)
-        src[k, 1] = masked(hphi, k)
-        out_copy(k).start()
-    each(1, n, send_out)
+    grids = (gridp, gridh)
+
+    def out_copy(i, k):
+        return to_group(src.at[k, i], grids[i].at[me], as_.at[k, i], ar.at[me, i], k)
+
+    def in_wait(i, k):
+        to_group(src.at[k, i], grids[i].at[k], as_.at[k, i], ar.at[k, i], k).wait_recv()
+
+    def send_out(i, ref):
+        def one(s):
+            k = up(s)
+            src[k, i] = masked(ref, k)
+            out_copy(i, k).start()
+        each(1, n, one)
+    send_out(1, hphi)
+    send_out(0, phi)
+    fetch.wait()
+    each(1, n, lambda s: in_wait(1, down(s)))
+
+    def image(a):
+        total = jnp.zeros((rows, depth), F32)
+        for j in range(nbr):
+            total = total + jnp.dot(ker[a, j], gridh[col[j, a]], preferred_element_type=F32)
+        kh[a] = total
+    each(0, n, image)
 
     def take_in(s):
         k = down(s)
-        to_group(src.at[k], grid.at[k], as_.at[k], ar.at[k], k).wait_recv()
+        in_wait(0, k)
         shifted(k)
     each(1, n, take_in)
 
@@ -94,20 +123,18 @@
 
     def partial(s):
         a = up(s)
-        left = grid[a, 0]
+        left = gridp[a]
         for j in range(nbr):
-            res = lax.dot_general(left, shift[col[a, j]], (((1,), (1,)), ((), ())),
+            res = lax.dot_general(left, shift[col[j, a]], (((1,), (1,)), ((), ())),
                                   preferred_element_type=F32)
             for i in range(nreg):
                 part[i % 2, i // 2, a, j] = res[i * slab:(i + 1) * slab]
         each(1, pairs + 1, lambda t: core_copy(qup(t), a).start())
-    each(1, n + 1, partial)
-
     def y_copy(p, a):
-        return to_region(part.at[c, p, a], ybuf.at[q, a], ys.at[p, a], yr.at[q, a], 2 * p + c)
+        return to_region(ysend.at[p, a], ybuf.at[q, a], ys.at[p, a], yr.at[q, a], 2 * p + c)
 
     def y_wait(p, a):
-        to_region(part.at[c, p, a], ybuf.at[p, a], ys.at[p, a], yr.at[p, a], 2 * p + c).wait_recv()
+        to_region(ysend.at[p, a], ybuf.at[p, a], ys.at[p, a], yr.at[p, a], 2 * p + c).wait_recv()
 
     def forward(s):
         a = up(s)
@@ -115,39 +142,43 @@
         def one(t):
             p = qup(t)
             core_copy(p, a).wait_recv()
-            part[c, p, a] = part[c, p, a] + cbuf[p, a]
+            ysend[p, a] = (part[c, p, a] + cbuf[p, a]).astype(BF16)
             y_copy(p, a).start()
         each(1, pairs, one)
-    each(1, n + 1, forward)
+
+    partial(1)
+
+    def both(s):
+        partial(s)
+        forward(s - 1)
+    each(2, n + 1, both)
+    forward(n)
 
     def red_copy(k):
-        return to_group(red.at[k], gbuf.at[me], gs.at[k], gr.at[me], k)
+        return to_group(rsend.at[k], gbuf.at[me], gs.at[k], gr.at[me], k)
 
     def reduce_one(a):
-        total = jnp.zeros((rows, depth), F32)
-        for j in range(nbr):
-            total = total + jnp.dot(ker[a, j], grid[col[a, j], 1], preferred_element_type=F32)
-        kh[a] = total
         core_copy(q, a).wait_recv()
         red[a] = part[c, q, a] + cbuf[q, a]
 
         def one(t):
             p = qup(t)
             y_wait(p, a)
-            red[a] = red[a] + ybuf[p, a]
+            red[a] = red[a] + ybuf[p, a].astype(F32)
         each(1, pairs, one)
 
     def reduce_send(s):
         a = up(s)
         reduce_one(a)
+        rsend[a] = red[a].astype(BF16)
         red_copy(a).start()
     each(1, n, reduce_send)
     reduce_one(me)
 
     def gather_sum(s):
         k = down(s)
-        to_group(red.at[k], gbuf.at[k], gs.at[k], gr.at[k], k).wait_recv()
-        red[me] = red[me] + gbuf[k]
+        to_group(rsend.at[k], gbuf.at[k], gs.at[k], gr.at[k], k).wait_recv()
+        red[me] = red[me] + gbuf[k].astype(F32)
     each(1, n, gather_sum)
 
     slot = lax.broadcasted_iota(jnp.int32, (nbr, slab, rows), 0)
@@ -182,6 +213,8 @@
         return to_region(fbuf.at[r], fbuf.at[r], fs.at[i], fr.at[r], i)
 
     each(1, n, lambda s: low_copy(up(s)).start())
+    each(1, pairs, lambda t: ly_copy(qup(t), me).start())
+    lc_copy(q, me).start()
 
     def spread(s):
         k = down(s)
@@ -189,8 +222,6 @@
         each(1, pairs, lambda t: ly_copy(qup(t), k).start())
         lc_copy(q, k).start()
     each(1, n, spread)
-    each(1, pairs, lambda t: ly_copy(qup(t), me).start())
-    lc_copy(q, me).start()
     each(1, nreg, lambda t: full_copy(rup(t)).start())
 
     def relay(s):
@@ -201,7 +232,7 @@
             ly_wait(p, k)
             lc_copy(p, k).start()
         each(1, pairs, one)
-    each(1, n + 1, relay)
+    relay(1)
 
     def back_copy(a):
         return to_group(shift.at[a], ret.at[me], bs.at[a], br.at[me], a)
@@ -211,10 +242,11 @@
         total = kh[a]
         for j in range(nbr):
             block = jnp.concatenate([low[i % 2, i // 2, a, j] for i in range(nreg)], axis=0)
-            total = total - jnp.dot(block, grid[col[a, j], 0], preferred_element_type=F32)
+            total = total - jnp.dot(block, gridp[col[j, a]], preferred_element_type=F32)
         return total.astype(BF16)
 
     def send_back(s):
+        relay(s + 1)
         a = down(s)
         shift[a] = descend(a)
         back_copy(a).start()
@@ -241,7 +273,8 @@
 
     def drain(s):
         k = up(s)
-        out_copy(k).wait_send()
+        out_copy(0, k).wait_send()
+        out_copy(1, k).wait_send()
         red_copy(k).wait_send()
         low_copy(k).wait_send()
         back_copy(k).wait_send()
@@ -271,27 +304,31 @@
     slab = rows // nreg
     dma = pltpu.SemaphoreType.DMA
     vmem = pl.BlockSpec(memory_space=pltpu.VMEM)
-    smem = pl.BlockSpec(memory_space=pltpu.SMEM)
     return pl.pallas_call(
         functools.partial(body, n, nreg),
         out_shape=(jax.ShapeDtypeStruct((rows, width), BF16),
                    jax.ShapeDtypeStruct((1, nbr, rows, rows), F32)),
-        in_specs=[vmem, vmem, vmem, smem, vmem],
+        in_specs=[vmem, vmem, vmem, pl.BlockSpec(memory_space=pl.ANY), vmem],
         out_specs=(vmem, vmem),
         scratch_shapes=[
+            pltpu.SMEM(columns.shape[::-1], jnp.int32),
+            dma(()),
+            pltpu.VMEM((pairs, n, nbr, slab, rows), BF16),
+            pltpu.VMEM((n, nbr, slab, rows), BF16),
             pltpu.VMEM((n, 2, rows, depth), BF16),
-            pltpu.VMEM((n, 2, rows, depth), BF16),
+            pltpu.VMEM((n, rows, depth), BF16),
+            pltpu.VMEM((n, rows, depth), BF16),
             pltpu.VMEM((n, rows, depth), BF16),
             pltpu.VMEM((2, pairs, n, nbr, slab, rows), F32),
             pltpu.VMEM((pairs, n, nbr, slab, rows), F32),
-            pltpu.VMEM((pairs, n, nbr, slab, rows), F32),
+            pltpu.VMEM((pairs, n, nbr, slab, rows), BF16),
             pltpu.VMEM((n, nbr, slab, rows), F32),
-            pltpu.VMEM((n, nbr, slab, rows), F32),
+            pltpu.VMEM((n, nbr, slab, rows), BF16),
             pltpu.VMEM((2, pairs, n, nbr, slab, rows), BF16),
             pltpu.VMEM((nreg, nbr, slab, rows), F32),
             pltpu.VMEM((n, rows, depth), F32),
             pltpu.VMEM((n, rows, depth), BF16),
-            dma((n,)), dma((n,)),
+            dma((n, 2)), dma((n, 2)),
             dma((pairs, n)), dma((pairs, n)),
             dma((pairs, n)), dma((pairs, n)),
             dma((n,)), dma((n,)),
@@ -306,7 +343,7 @@
         cost_estimate=pl.CostEstimate(
             flops=6 * n * nbr * rows * rows * depth, bytes_accessed=8 * rows * width,
             transcendentals=0),
-    )(phi, hphi, extents, columns, kernel)
+    )(phi, hphi, extents.T, columns.T, kernel)
 
 
 def solution(mesh):

time: 98.7 us -> 88 us (0.89)
  the two profiles are of different devices: /device:TPU:0 before, /device:TPU:2 now
where the time goes in v2:
time: 88 us; the launch traced here: 87.8 us
  Pallas kernels  84.4 us (96%)
  local copies, waits for them, and re-layouts  2.78 us (3%)
    pallas_call x1, Pallas kernels, shards(): pl.pallas_call(functools.partial(body, n, nreg), out_shape=(jax.ShapeDtyp...  84.4 us
    unnamed x4, local copies, waits for them, and re-layouts  2.78 us

profile of v2, /device:TPU:2, one launch (start us, length us, event | category | flops | bytes accessed | tf_op | source)
XLA Modules:
  0.0 87.8 jit_solution(1261010461090193473)
XLA Ops:
  0.6 84.4 %shard_map.68 = (bf16[128,3072]{1,0:T(8,128)(2,1)}, f32[1,3,128,128]{3,2,1,0:T(8,128)}) custom-call(bf16[128,3072]{1,0:T(8,128)(2,1)} %phi.1, bf16[128,3072]{1,0:T(8,128)(2,1)} %hphi.1, s32[2,128]{1,0:T(2,128)} %bitcast.3, s32[3,8]{1,0:T(4,128)} %bitcast.2, bf16[8,3,128,128]{3,2,1,0:T(8,128)(2,1)} %ker.1), custom_call_target="tpu_custom_call" | custom-call | flops 905969664 | bytes 3145728 | tf_op jit(solution)/shard_map/pallas_call | solution.py:307
  85.0 0.0 copy-start
  85.0 2.1 %copy.9 = bf16[128,3072]{1,0:T(8,128)(2,1)} copy(bf16[128,3072]{1,0:T(8,128)(2,1)} %get-tuple-element.4) | data formatting | bytes 1572864
  87.1 0.0 copy-done
  87.1 0.7 copy.10
Async XLA Ops:
  85.0 2.1 %copy-start = (f32[1,3,128,128]{3,2,1,0:T(8,128)S(1)}, f32[1,3,128,128]{3,2,1,0:T(8,128)}, u32[]{:S(2)}) copy-start(f32[1,3,128,128]{3,2,1,0:T(8,128)} %get-tuple-element.5) | copy-start | bytes 589828

commit v3 on v2

--- a/solution.py
+++ b/solution.py
@@ -42,16 +42,16 @@
         lax.fori_loop(lo, hi, step, 0)
 
     half = n // 2
-    base = me // half * half
-    place = me % half
 
     def up(s):
-        start = jnp.where(s <= half, half - base, base)
-        return start + lax.rem(place + jnp.where(s <= half, s - 1, s - half), half)
-
-    def down(s):
-        start = jnp.where(s <= half, half - base, base)
-        return start + lax.rem(place + n - jnp.where(s <= half, s - 1, s - half), half)
+        turn = s // 2 % half + s % 2 * half
+        total, bit = 0, 1
+        while bit < n:
+            total = total + (me // bit + turn // bit) % 2 * bit
+            bit = 2 * bit
+        return total
+
+    down = up
 
     rup = lambda t: lax.rem(r + t, nreg)
     qup = lambda t: lax.rem(q + t, pairs)

time: 88 us -> 85.9 us (0.976)
  the two profiles are of different devices: /device:TPU:2 before, /device:TPU:0 now
where the time goes in v3:
time: 85.9 us; the launch traced here: 84.5 us
  Pallas kernels  81.1 us (94%)
  local copies, waits for them, and re-layouts  2.78 us (3%)
    pallas_call x1, Pallas kernels, shards(): pl.pallas_call(functools.partial(body, n, nreg), out_shape=(jax.ShapeDtyp...  81.1 us
    unnamed x4, local copies, waits for them, and re-layouts  2.78 us

profile of v3, /device:TPU:0, one launch (start us, length us, event | category | flops | bytes accessed | tf_op | source)
XLA Modules:
  0.0 84.5 jit_solution(12925249964564774468)
XLA Ops:
  0.6 81.1 %shard_map.68 = (bf16[128,3072]{1,0:T(8,128)(2,1)}, f32[1,3,128,128]{3,2,1,0:T(8,128)}) custom-call(bf16[128,3072]{1,0:T(8,128)(2,1)} %phi.1, bf16[128,3072]{1,0:T(8,128)(2,1)} %hphi.1, s32[2,128]{1,0:T(2,128)} %bitcast.3, s32[3,8]{1,0:T(4,128)} %bitcast.2, bf16[8,3,128,128]{3,2,1,0:T(8,128)(2,1)} %ker.1), custom_call_target="tpu_custom_call" | custom-call | flops 905969664 | bytes 3145728 | tf_op jit(solution)/shard_map/pallas_call | solution.py:307
  81.7 0.0 copy-start
  81.7 2.1 %copy.9 = bf16[128,3072]{1,0:T(8,128)(2,1)} copy(bf16[128,3072]{1,0:T(8,128)(2,1)} %get-tuple-element.4) | data formatting | bytes 1572864
  83.8 0.0 copy-done
  83.8 0.7 copy.10
Async XLA Ops:
  81.7 2.1 %copy-start = (f32[1,3,128,128]{3,2,1,0:T(8,128)S(1)}, f32[1,3,128,128]{3,2,1,0:T(8,128)}, u32[]{:S(2)}) copy-start(f32[1,3,128,128]{3,2,1,0:T(8,128)} %get-tuple-element.5) | copy-start | bytes 589828
